TPU v7x, 32 devices: a whole 2x2x4 slice. The times are simulated.
32 devices in a mesh: mem: 4 (over y, x), reg: 8 (over z, core).
Axes of the slice: x: 2, y: 2, z: 4, core: 2. Of those that a mesh axis runs over, the one named last changes fastest.
Arguments:
- prior_states: bfloat16 [256, 227, 1024], P('mem', None, 'reg'), may hold values from -6 to 6
- sensor_space_runs: bfloat16 [256, 8, 8192], P('mem', 'reg'), may hold values from -6 to 6
- sensor_readings: float32 [8, 8192], P('reg'), may hold values from -8 to 8
- noise_precision: float32 [8, 8192], P('reg'), may hold values from 0.1 to 1
- reading_pointers: int32 [8, 4, 4, 512], P('reg', 'mem'), may hold values from 0 to 8703, as said below
- reading_tally: int32 [8, 4, 4], P('reg', 'mem'), may hold values from 128 to 512, as said below
Outputs:
- analysis: bfloat16 [256, 227, 1024], P('mem', None, 'reg')
Inputs may be any that keep to these rules, and one draw needn't show every extreme that they name: Row reading_pointers[r, m, g, :] holds 512 distinct positions of region r's extended observations, together one window of 512 consecutive positions, in an order drawn from the seed. A local analysis uses the first reading_tally[r, m, g] entries of its list.
All inputs are finite; a program needn't handle non-finite values.
Results may differ from a plain program's by a relative error of at most 0.009.
Values may be sent and summed in bfloat16 or wider, within the bound.
A program may use at most 128 MiB of HBM per device.

v0:
```python
import functools
import math

import jax
import jax.numpy as jnp
from jax import lax
from jax.experimental import pallas as pl
from jax.experimental.pallas import tpu as pltpu
from jax.sharding import PartitionSpec as P

NS_ITERS = 6
HW = 256
LANES = 128
CHUNKS = 4
VMEM_LIMIT = 60 * 1024 * 1024

inflation = 1.1
highest = lax.Precision.HIGHEST
MESH = pl.DeviceIdType.MESH


def lane_part(shape, width):
    return lax.broadcasted_iota(jnp.int32, shape, len(shape) - 1) // width


def swap_lane_parts(pieces, width):
    parts = len(pieces)
    part = lane_part(pieces[0].shape, width)
    swapped = []
    for d in range(parts):
        result = pieces[d]
        for s in range(parts):
            if s != d:
                moved = pltpu.roll(pieces[s], (s - d) * width % LANES, 1)
                result = jnp.where(part == s, moved, result)
        swapped.append(result)
    return swapped


def pack_kernel(states_ref, packed_ref):
    fields, _, columns = states_ref.shape
    blocks, rows, _, _ = packed_ref.shape
    width = columns // blocks
    parts = LANES // width

    def body(r, carry):
        for tile in range(columns // LANES):
            lanes = slice(tile * LANES, (tile + 1) * LANES)
            pieces = [
                states_ref[jnp.minimum(s * rows + r, fields - 1), :, lanes].astype(jnp.float32)
                for s in range(parts)
            ]
            for d, piece in enumerate(swap_lane_parts(pieces, width)):
                packed_ref[tile * parts + d, r] = piece.astype(jnp.bfloat16)
        return carry

    lax.fori_loop(0, rows, body, 0)


def pack(states, blocks):
    fields, runs, columns = states.shape
    rows = -(-fields // (LANES // (columns // blocks)))
    return pl.pallas_call(
        pack_kernel,
        out_shape=jax.ShapeDtypeStruct((blocks, rows, runs, LANES), jnp.bfloat16),
        in_specs=[pl.BlockSpec(memory_space=pltpu.VMEM)],
        out_specs=pl.BlockSpec(memory_space=pltpu.VMEM),
        compiler_params=pltpu.CompilerParams(vmem_limit_bytes=VMEM_LIMIT),
        name="pack_columns",
    )(states)


def window_kernel(starts_ref, before_ref, own_ref, after_ref, windows_ref, extended):
    width = before_ref.shape[1]
    own = own_ref.shape[1]
    length = windows_ref.shape[2]
    extended[:, :width] = before_ref[...]
    extended[:, width : width + own] = own_ref[...]
    extended[:, width + own :] = after_ref[...]
    span = length + LANES
    last = extended.shape[1] - span

    def body(w, carry):
        start = starts_ref[w]
        base = pl.multiple_of(jnp.minimum(start // LANES * LANES, last), LANES)
        wide = extended[:, pl.ds(base, span)].astype(jnp.float32)
        turned = pltpu.roll(wide, lax.rem(span - (start - base), span), 1)
        windows_ref[w] = turned[:, :length].astype(jnp.bfloat16)
        return carry

    lax.fori_loop(0, windows_ref.shape[0], body, 0)


def cut_windows(starts, before, own, after, length):
    runs, own_width = own.shape
    return pl.pallas_call(
        window_kernel,
        out_shape=jax.ShapeDtypeStruct((starts.shape[0], runs, length), jnp.bfloat16),
        in_specs=[pl.BlockSpec(memory_space=pltpu.SMEM)]
        + [pl.BlockSpec(memory_space=pltpu.VMEM)] * 3,
        out_specs=pl.BlockSpec(memory_space=pltpu.VMEM),
        scratch_shapes=[pltpu.VMEM((runs, own_width + 2 * before.shape[1]), jnp.bfloat16)],
        compiler_params=pltpu.CompilerParams(vmem_limit_bytes=VMEM_LIMIT),
        name="cut_windows",
    )(starts, before, own, after)


def chunk_bounds(rows):
    edges = [rows * i // CHUNKS for i in range(CHUNKS + 1)]
    return list(zip(edges[:-1], edges[1:]))


def apply_rows(transform_ref, states_ref, result_ref, first, last, patch, groups):
    blocks, _, runs, _ = states_ref.shape
    members = blocks * runs

    def one(r):
        x = jnp.concatenate([states_ref[b, r] for b in range(blocks)], axis=0)
        x = x.astype(jnp.float32)
        center = jnp.sum(x, axis=0, keepdims=True) * (1.0 / members)
        pert = (x - center).astype(jnp.bfloat16).astype(jnp.float32)
        group = lane_part(pert.shape, patch) % groups
        masked = [jnp.where(group == g, pert, 0.0).astype(jnp.bfloat16) for g in range(groups)]
        return center, jnp.concatenate(masked, axis=0)

    def body(i, carry):
        r0 = first + 2 * i
        r1 = jnp.minimum(r0 + 1, last - 1)
        center0, masked0 = one(r0)
        center1, masked1 = one(r1)
        moved = jnp.dot(
            transform_ref[...],
            jnp.concatenate([masked0, masked1], axis=1),
            preferred_element_type=jnp.float32,
        )
        for r, center, lanes in ((r0, center0, slice(0, LANES)), (r1, center1, slice(LANES, None))):
            analysed = (moved[:, lanes] + center).astype(jnp.bfloat16)
            for b in range(blocks):
                result_ref[b, r] = analysed[b * runs : (b + 1) * runs]
        return carry

    lax.fori_loop(0, (last - first + 1) // 2, body, 0)


def unpack_row(received, result_ref, r, valid):
    blocks, rows, _, _ = received.shape
    columns = result_ref.shape[2]
    width = columns // blocks
    parts = LANES // width
    for tile in range(columns // LANES):
        lanes = slice(tile * LANES, (tile + 1) * LANES)
        pieces = [received[tile * parts + d, r].astype(jnp.float32) for d in range(parts)]
        swapped = swap_lane_parts(pieces, width)
        for s in range(valid):
            result_ref[s * rows + r, :, lanes] = swapped[s].astype(jnp.bfloat16)


def unpack_rows(received, result_ref, first, last):
    rows = received.shape[1]
    fields = result_ref.shape[0]
    parts = LANES // (result_ref.shape[2] // received.shape[0])
    whole = rows - (parts * rows - fields)

    def body(r, carry):
        unpack_row(received, result_ref, r, parts)
        return carry

    lax.fori_loop(first, min(last, whole), body, 0)
    for r in range(max(first, whole), last):
        unpack_row(received, result_ref, r, parts - 1)


def analysis_kernel(
    patch, groups, transform_ref, states_ref, result_ref, outgoing, received, send_sem, recv_sem
):
    blocks, rows, _, _ = states_ref.shape
    me = lax.axis_index("mem")
    barrier = pltpu.get_barrier_semaphore()
    for k in range(1, blocks):
        pl.semaphore_signal(
            barrier, inc=1, device_id={"mem": lax.rem(me + k, blocks)}, device_id_type=MESH
        )
    pl.semaphore_wait(barrier, blocks - 1)

    copies = []
    for c, (first, last) in enumerate(chunk_bounds(rows)):
        apply_rows(transform_ref, states_ref, outgoing, first, last, patch, groups)
        started = []
        for k in range(1, blocks):
            peer = lax.rem(me + k, blocks)
            copy = pltpu.make_async_remote_copy(
                src_ref=outgoing.at[peer, pl.ds(first, last - first)],
                dst_ref=received.at[me, pl.ds(first, last - first)],
                send_sem=send_sem.at[k - 1, c],
                recv_sem=recv_sem.at[k - 1, c],
                device_id={"mem": peer},
                device_id_type=MESH,
            )
            copy.start()
            started.append(copy)
        received[me, pl.ds(first, last - first)] = outgoing[me, pl.ds(first, last - first)]
        copies.append(started)
    for (first, last), started in zip(chunk_bounds(rows), copies):
        for copy in started:
            copy.wait_recv()
        unpack_rows(received, result_ref, first, last)
    for started in copies:
        for copy in started:
            copy.wait_send()


def analyse(transform, states, fields, columns, patch, groups):
    blocks, rows, runs, _ = states.shape
    return pl.pallas_call(
        functools.partial(analysis_kernel, patch, groups),
        out_shape=jax.ShapeDtypeStruct((fields, runs, columns), jnp.bfloat16),
        in_specs=[pl.BlockSpec(memory_space=pltpu.VMEM)] * 2,
        out_specs=pl.BlockSpec(memory_space=pltpu.VMEM),
        scratch_shapes=[
            pltpu.VMEM(states.shape, jnp.bfloat16),
            pltpu.VMEM(states.shape, jnp.bfloat16),
            pltpu.SemaphoreType.DMA((blocks - 1, CHUNKS)),
            pltpu.SemaphoreType.DMA((blocks - 1, CHUNKS)),
        ],
        compiler_params=pltpu.CompilerParams(
            collective_id=0, has_side_effects=True, vmem_limit_bytes=VMEM_LIMIT
        ),
        name="analyse_and_return",
    )(transform, states)


def from_neighbours(cells, width):
    count = lax.axis_size("reg")
    head, tail = cells[:, :width], cells[:, cells.shape[1] - width :]
    before = lax.ppermute(tail, "reg", [(i, (i + 1) % count) for i in range(count)])
    after = lax.ppermute(head, "reg", [((i + 1) % count, i) for i in range(count)])
    return before, after


def local_transform(lines, readings, weight):
    members = lines.shape[0]
    observed = lines.astype(jnp.float32)
    ens_mean = jnp.mean(observed, axis=0)
    anomaly = lax.optimization_barrier((observed - ens_mean[None]).astype(jnp.bfloat16)).astype(
        jnp.float32
    )
    identity = jnp.eye(members, dtype=jnp.float32)
    gram = (
        jnp.dot(anomaly, (anomaly * weight[None, :]).T, precision=highest)
        + (members - 1) / inflation * identity
    )
    innovation_sum = jnp.dot(anomaly, weight * (readings - ens_mean), precision=highest)
    frobenius = jnp.sqrt(jnp.sum(gram * gram))
    iterate = gram / frobenius
    dot = functools.partial(jnp.dot, precision=lax.Precision.HIGH)
    factor = 1.5 * identity - 0.5 * iterate
    inverse_root = factor
    for iteration in range(1, NS_ITERS):
        iterate = dot(iterate, factor)
        factor = 1.5 * identity - 0.5 * dot(inverse_root, iterate)
        inverse_root = dot(factor, inverse_root)
    inverse_root = inverse_root / jnp.sqrt(frobenius)
    mean_weight = jnp.dot(
        inverse_root, jnp.dot(inverse_root, innovation_sum, precision=highest), precision=highest
    )
    transform = math.sqrt(members - 1) * inverse_root + mean_weight[:, None]
    return transform.astype(jnp.bfloat16).T


def per_device(
    prior_states,
    sensor_space_runs,
    sensor_readings,
    noise_precision,
    reading_pointers,
    reading_tally,
):
    blocks = lax.axis_size("mem")
    runs, fields, columns = prior_states.shape
    members = runs * blocks
    groups = reading_tally.shape[2]
    patch = columns // blocks // groups
    packed = pack(jnp.transpose(prior_states, (1, 0, 2)), blocks)
    states = lax.all_to_all(packed, "mem", split_axis=0, concat_axis=0, tiled=True)

    lists = reading_pointers[0, 0]
    length = lists.shape[1]
    starts = jnp.min(lists, axis=1)
    all_starts = lax.all_gather(starts, "mem", axis=0, tiled=True)
    own_runs = sensor_space_runs[:, 0]
    before, after = from_neighbours(own_runs, HW)
    windows = cut_windows(all_starts, before, own_runs, after, length)
    windows = lax.all_to_all(windows, "mem", split_axis=0, concat_axis=0, tiled=True)
    lines = windows.reshape(blocks, groups, runs, length).transpose(1, 0, 2, 3)
    lines = lines.reshape(groups, members, length)

    statistics = jnp.concatenate([sensor_readings, noise_precision])
    stats_before, stats_after = from_neighbours(statistics, HW)
    statistics = jnp.concatenate([stats_before, statistics, stats_after], axis=1)
    moments = jnp.stack(
        [lax.dynamic_slice_in_dim(statistics, starts[g], length, axis=1) for g in range(groups)]
    )
    places = jnp.arange(length, dtype=jnp.int32)
    used = places[None, :] < reading_tally[0, 0][:, None]
    active = jnp.any(
        ((lists - starts[:, None])[:, :, None] == places[None, None, :]) & used[:, :, None], axis=1
    )
    weight = moments[:, 1] * active.astype(jnp.float32)
    turned = jax.vmap(local_transform)(lines, moments[:, 0], weight)
    transform = turned.transpose(1, 0, 2).reshape(members, groups * members)
    transform, states = lax.optimization_barrier((transform, states))
    analysed = analyse(transform, states, fields, columns, patch, groups)
    return jnp.transpose(analysed, (1, 0, 2))


def solution(mesh):
    placed = (
        P("mem", None, "reg"),
        P("mem", "reg", None),
        P("reg", None),
        P("reg", None),
        P("reg", "mem", None, None),
        P("reg", "mem", None),
    )
    return jax.shard_map(
        per_device, mesh=mesh, in_specs=placed, out_specs=P("mem", None, "reg"), check_vma=False
    )
```

profile of v0, /device:TPU:0, one launch (start us, length us, event | category | flops | bytes accessed | tf_op | source)
XLA Modules:
  0.0 161.7 jit_solution(16166987944020817438)
XLA Ops:
  0.0 0.7 pad_maximum_fusion.3
  1.2 4.1 %collective-permute-start.3 = (f32[2,256]{1,0:T(2,128)S(1)}, f32[2,256]{1,0:T(2,128)S(1)}, u32[]{:S(2)}, u32[]{:S(2)}) collective-permute-start(f32[2,256]{1,0:T(2,128)S(1)} %get-tuple-element.16), channel_id=1, source_target_pairs={{1,0},{2,1},{3,2},{4,3},{5,4},{6,5},{7,6},{0,7},{9,8},{10,9},{11,1... | collective-permute-start | bytes 6152 | tf_op jit(solution)/shard_map/ppermute | solution.py:236
  5.3 0.8 fusion.37
  6.8 0.7 iota_compare_fusion.2
  7.6 0.8 reduce_min.9
  8.4 0.8 bitcast_subtract_fusion.1
  9.2 1.2 dynamic-slice
  11.3 0.7 fusion.1
  12.7 8.2 %all-reduce.starts_ref = s32[16]{0:T(128)} all-reduce(s32[16]{0:T(128)S(1)} %dynamic-update-slice), channel_id=1, replica_groups=mesh['mem'=4,'reg'=8] {'mem'}, use_global_device_ids=true, to_apply=%add | all-reduce | flops 16 | bytes 128
  25.7 10.8 %pack_columns.1 = bf16[4,57,64,128]{3,2,1,0:T(8,128)(2,1)} custom-call(bf16[227,64,128]{2,1,0:T(8,128)(2,1)} %bitcast.82), custom_call_target="tpu_custom_call" | custom-call | tf_op jit(solution)/shard_map/pack_columns/pallas_call | solution.py:63
  40.1 4.3 %cut_windows.1 = bf16[16,64,512]{2,1,0:T(8,128)(2,1)} custom-call(s32[16]{0:T(128)} %all-reduce.starts_ref, bf16[64,256]{1,0:T(8,128)(2,1)} %copy-done.3, bf16[64,8192]{1,0:T(8,128)(2,1)} %bitcast.85, bf16[64,256]{1,0:T(8,128)(2,1)} %copy-done.2), custom_call_target="tpu_custom_call" | custom-call | tf_op jit(solution)/shard_map/cut_windows/pallas_call | solution.py:96
  44.4 3.5 %all-to-all-start = ((bf16[16,64,512]{2,1,0:T(8,128)(2,1)}), bf16[16,64,512]{2,1,0:T(8,128)(2,1)S(1)}, u32[]{:S(2)}, u32[]{:S(2)}) async-start(bf16[16,64,512]{2,1,0:T(8,128)(2,1)} %cut_windows.1), calls=%async_computation | async-start | bytes 2097152 | tf_op jit(solution)/shard_map/all_to_all | solution.py:293
  48.2 11.7 %all-to-all-done = bf16[16,64,512]{2,1,0:T(8,128)(2,1)S(1)} async-done(((bf16[16,64,512]{2,1,0:T(8,128)(2,1)}), bf16[16,64,512]{2,1,0:T(8,128)(2,1)S(1)}, u32[]{:S(2)}, u32[]{:S(2)}) %all-to-all-start) | async-done | bytes 1048608 | tf_op jit(solution)/shard_map/all_to_all | solution.py:293
  59.9 4.8 %all-to-all-start.1 = ((bf16[4,57,64,128]{3,2,1,0:T(8,128)(2,1)}), bf16[4,57,64,128]{3,2,1,0:T(8,128)(2,1)}, u32[]{:S(2)}, u32[]{:S(2)}) async-start(bf16[4,57,64,128]{3,2,1,0:T(8,128)(2,1)} %pack_columns.1), calls=%async_computation.1 | async-start | bytes 7471104 | tf_op jit(solution)/shard_map/all_to_all | solution.py:284
  65.8 1.5 multiply_reduce_fusion
  67.3 0.8 fusion.15
  68.1 0.8 fusion.13
  68.9 0.8 fusion.14
  69.7 0.7 fusion.39
  70.4 0.7 fusion.12
  72.5 0.9 fusion.28
  73.4 0.7 fusion.11
  75.6 0.7 fusion.10
  76.3 0.7 fusion.44
  77.7 0.7 fusion.9
  78.4 0.9 convolution_divide_fusion
  79.3 1.0 fusion.32
  80.3 1.0 fusion.30
  81.5 1.0 copy.18.transform_ref
  82.5 24.1 %all-to-all-done.1.states_ref = bf16[4,57,64,128]{3,2,1,0:T(8,128)(2,1)} async-done(((bf16[4,57,64,128]{3,2,1,0:T(8,128)(2,1)}), bf16[4,57,64,128]{3,2,1,0:T(8,128)(2,1)}, u32[]{:S(2)}, u32[]{:S(2)}) %all-to-all-start.1) | async-done | bytes 3735584 | tf_op jit(solution)/shard_map/all_to_all | solution.py:284
  106.6 50.3 %analyse_and_return.1 = bf16[227,64,128]{2,1,0:T(8,128)(2,1)} custom-call(bf16[256,1024]{1,0:T(8,128)(2,1)} %copy.18.transform_ref, bf16[4,57,64,128]{3,2,1,0:T(8,128)(2,1)} %all-to-all-done.1.states_ref), custom_call_target="tpu_custom_call" | custom-call | tf_op jit(solution)/shard_map/analyse_and_return/pallas_call | solution.py:214
  156.9 4.7 %copy.33 = bf16[64,227,128]{2,0,1:T(8,128)(2,1)} copy(bf16[64,227,128]{2,0,1:T(8,128)(2,1)} %bitcast.80) | data formatting | bytes 7438336
  (45 shorter events, 8.2 us)
Async XLA Ops:
  0.7 47.2 %collective-permute-start.2 = (f32[2,256]{1,0:T(2,128)S(1)}, f32[2,256]{1,0:T(2,128)S(1)}, u32[]{:S(2)}, u32[]{:S(2)}) collective-permute-start(f32[2,256]{1,0:T(2,128)S(1)} %get-tuple-element.15), channel_id=1, source_target_pairs={{0,1},{1,2},{2,3},{3,4},{4,5},{5,6},{6,7},{7,0},{8,9},{9,10},{10,1... | collective-permute-start | bytes 6152 | tf_op jit(solution)/shard_map/ppermute | solution.py:235
  1.2 46.7 %collective-permute-start.3 = (f32[2,256]{1,0:T(2,128)S(1)}, f32[2,256]{1,0:T(2,128)S(1)}, u32[]{:S(2)}, u32[]{:S(2)}) collective-permute-start(f32[2,256]{1,0:T(2,128)S(1)} %get-tuple-element.16), channel_id=1, source_target_pairs={{1,0},{2,1},{3,2},{4,3},{5,4},{6,5},{7,6},{0,7},{9,8},{10,9},{11,1... | collective-permute-start | bytes 6152 | tf_op jit(solution)/shard_map/ppermute | solution.py:236
  6.1 32.8 %collective-permute-start.1 = (bf16[64,256]{1,0:T(8,128)(2,1)S(1)}, bf16[64,256]{1,0:T(8,128)(2,1)S(1)}, u32[]{:S(2)}, u32[]{:S(2)}) collective-permute-start(bf16[64,256]{1,0:T(8,128)(2,1)S(1)} %get-tuple-element.9), channel_id=1, source_target_pairs={{1,0},{2,1},{3,2},{4,3},{5,4},{6,5},{7,6},{0,7},{9,8},{10,9},{11,1... | collective-permute-start | bytes 98312 | tf_op jit(solution)/shard_map/ppermute | solution.py:236
  6.8 32.1 %collective-permute-start = (bf16[64,256]{1,0:T(8,128)(2,1)S(1)}, bf16[64,256]{1,0:T(8,128)(2,1)S(1)}, u32[]{:S(2)}, u32[]{:S(2)}) collective-permute-start(bf16[64,256]{1,0:T(8,128)(2,1)S(1)} %get-tuple-element.10), channel_id=1, source_target_pairs={{0,1},{1,2},{2,3},{3,4},{4,5},{5,6},{6,7},{7,0},{8,9},{9,10},{10,1... | collective-permute-start | bytes 98312 | tf_op jit(solution)/shard_map/ppermute | solution.py:235
  38.9 9.1 %copy-start = (f32[1,8192]{1,0:T(1,128)S(1)}, f32[1,8192]{1,0:T(1,128)}, u32[]{:S(2)}) copy-start(f32[1,8192]{1,0:T(1,128)} %param.9) | copy-start | bytes 98308
  38.9 9.1 %copy-start.1 = (f32[1,8192]{1,0:T(1,128)S(1)}, f32[1,8192]{1,0:T(1,128)}, u32[]{:S(2)}) copy-start(f32[1,8192]{1,0:T(1,128)} %param.8) | copy-start | bytes 98308
  38.9 0.6 copy-start.2
  39.5 0.6 copy-start.3
  44.4 15.6 %all-to-all-start = ((bf16[16,64,512]{2,1,0:T(8,128)(2,1)}), bf16[16,64,512]{2,1,0:T(8,128)(2,1)S(1)}, u32[]{:S(2)}, u32[]{:S(2)}) async-start(bf16[16,64,512]{2,1,0:T(8,128)(2,1)} %cut_windows.1), calls=%async_computation | async-start | bytes 2097152 | tf_op jit(solution)/shard_map/all_to_all | solution.py:293
  59.9 46.7 %all-to-all-start.1 = ((bf16[4,57,64,128]{3,2,1,0:T(8,128)(2,1)}), bf16[4,57,64,128]{3,2,1,0:T(8,128)(2,1)}, u32[]{:S(2)}, u32[]{:S(2)}) async-start(bf16[4,57,64,128]{3,2,1,0:T(8,128)(2,1)} %pack_columns.1), calls=%async_computation.1 | async-start | bytes 7471104 | tf_op jit(solution)/shard_map/all_to_all | solution.py:284
where the time goes:
time: 162 us
  Pallas kernels  65.4 us (40%)
  waiting for transfers between devices  35.8 us (22%)
  matrix products  15.4 us (10%)
  starting transfers between devices  13.5 us (8%)
  local copies, waits for them, and re-layouts  10.2 us (6%)
  blocking collectives  8.23 us (5%)
  between operations  8.17 us (5%)
  other arithmetic  4.92 us (3%)
    pallas_call x1, Pallas kernels, analyse(): pl.pallas_call(functools.partial(analysis_kernel, patch, groups), out_sha...  50.3 us
    all_to_all x1, waiting for transfers between devices, per_device(): lax.all_to_all(packed, 'mem', split_axis=0, concat_axis=0, tiled=True)  24.1 us
    all_to_all x1, waiting for transfers between devices, per_device(): lax.all_to_all(windows, 'mem', split_axis=0, concat_axis=0, tiled=True)  11.7 us
    pallas_call x1, Pallas kernels, pack(): pl.pallas_call(pack_kernel, out_shape=jax.ShapeDtypeStruct((blocks, rows,...  10.8 us
    unnamed x1, blocking collectives  8.23 us
    unnamed x12, local copies, waits for them, and re-layouts  7.42 us
    ppermute x2, starting transfers between devices, from_neighbours(): lax.ppermute(head, 'reg', [((i + 1) % count, i) for i in range(count)])  4.78 us
    all_to_all x1, starting transfers between devices, per_device(): lax.all_to_all(packed, 'mem', split_axis=0, concat_axis=0, tiled=True)  4.75 us
  transfers between devices with their start and end apart: 6, of which 2 were waited for; matrix products, arithmetic and copies ran while one was open for 15% of the time, Pallas kernels for 9%

commit v1 on v0

v1 whole, which is shorter than its diff:
```python
import functools
import math

import jax
import jax.numpy as jnp
from jax import lax
from jax.experimental import pallas as pl
from jax.experimental.pallas import tpu as pltpu
from jax.sharding import PartitionSpec as P

NS_ITERS = 6
HW = 256
LANES = 128
CHUNKS = 4
VMEM_LIMIT = 60 * 1024 * 1024

inflation = 1.1
MESH = pl.DeviceIdType.MESH


def lane_part(shape, width):
    return lax.broadcasted_iota(jnp.int32, shape, len(shape) - 1) // width


def swap_lane_parts(pieces, width):
    parts = len(pieces)
    part = lane_part(pieces[0].shape, width)
    swapped = []
    for d in range(parts):
        result = pieces[d]
        for s in range(parts):
            if s != d:
                moved = pltpu.roll(pieces[s], (s - d) * width % LANES, 1)
                result = jnp.where(part == s, moved, result)
        swapped.append(result)
    return swapped


def chunk_bounds(rows):
    edges = [rows * i // CHUNKS for i in range(CHUNKS + 1)]
    return list(zip(edges[:-1], edges[1:]))


def apply_rows(transform_ref, states_ref, result_ref, first, last, patch, groups):
    blocks, _, runs, _ = states_ref.shape
    members = blocks * runs

    def one(r):
        x = jnp.concatenate([states_ref[b, r] for b in range(blocks)], axis=0)
        x = x.astype(jnp.float32)
        center = jnp.sum(x, axis=0, keepdims=True) * (1.0 / members)
        pert = (x - center).astype(jnp.bfloat16).astype(jnp.float32)
        group = lane_part(pert.shape, patch) % groups
        masked = [jnp.where(group == g, pert, 0.0).astype(jnp.bfloat16) for g in range(groups)]
        return center, jnp.concatenate(masked, axis=0)

    def body(i, carry):
        r0 = first + 2 * i
        r1 = jnp.minimum(r0 + 1, last - 1)
        center0, masked0 = one(r0)
        center1, masked1 = one(r1)
        moved = jnp.dot(
            transform_ref[...],
            jnp.concatenate([masked0, masked1], axis=1),
            preferred_element_type=jnp.float32,
        )
        for r, center, lanes in ((r0, center0, slice(0, LANES)), (r1, center1, slice(LANES, None))):
            analysed = (moved[:, lanes] + center).astype(jnp.bfloat16)
            for b in range(blocks):
                result_ref[b, r] = analysed[b * runs : (b + 1) * runs]
        return carry

    lax.fori_loop(0, (last - first + 1) // 2, body, 0)


def unpack_row(received, result_ref, r, valid):
    blocks, rows, _, _ = received.shape
    columns = result_ref.shape[2]
    width = columns // blocks
    parts = LANES // width
    for tile in range(columns // LANES):
        lanes = slice(tile * LANES, (tile + 1) * LANES)
        pieces = [received[tile * parts + d, r].astype(jnp.float32) for d in range(parts)]
        swapped = swap_lane_parts(pieces, width)
        for s in range(valid):
            result_ref[s * rows + r, :, lanes] = swapped[s].astype(jnp.bfloat16)


def unpack_rows(received, result_ref, first, last):
    rows = received.shape[1]
    fields = result_ref.shape[0]
    parts = LANES // (result_ref.shape[2] // received.shape[0])
    whole = rows - (parts * rows - fields)

    def body(r, carry):
        unpack_row(received, result_ref, r, parts)
        return carry

    lax.fori_loop(first, min(last, whole), body, 0)
    for r in range(max(first, whole), last):
        unpack_row(received, result_ref, r, parts - 1)


def pack_rows(states_ref, packed, first, last):
    fields, _, columns = states_ref.shape
    blocks, rows, _, _ = packed.shape
    width = columns // blocks
    parts = LANES // width

    def body(r, carry):
        for tile in range(columns // LANES):
            lanes = slice(tile * LANES, (tile + 1) * LANES)
            pieces = [
                states_ref[jnp.minimum(s * rows + r, fields - 1), :, lanes].astype(jnp.float32)
                for s in range(parts)
            ]
            for d, piece in enumerate(swap_lane_parts(pieces, width)):
                packed[tile * parts + d, r] = piece.astype(jnp.bfloat16)
        return carry

    lax.fori_loop(first, last, body, 0)


def bit_of(start, bit, shape, kind):
    value = jnp.broadcast_to((start >> bit) & 1, shape)
    return value.astype(jnp.float32).astype(kind) > 0.5


def nearest_tiles(extended, start, length):
    shape = (extended.shape[0], LANES)
    keep = length // LANES
    total = extended.shape[1] // LANES
    tiles = [extended[:, i * LANES : (i + 1) * LANES] for i in range(total)]
    for bit in reversed(range((total - keep).bit_length())):
        shift = 1 << bit
        mask = bit_of(start, bit + LANES.bit_length() - 1, shape, extended.dtype)
        tiles = [
            jnp.where(mask, tiles[i + shift], tiles[i]) if i + shift < len(tiles) else tiles[i]
            for i in range(min(len(tiles), shift + keep))
        ]
    return tiles


def load_runs(extended, start, length):
    tiles = nearest_tiles(extended, start, length)
    count = extended.shape[0]
    shape = (2 * LANES, LANES)
    row = lax.broadcasted_iota(jnp.int32, shape, 0)
    lane = lax.broadcasted_iota(jnp.int32, shape, 1)
    chosen = (row - lane == jnp.broadcast_to(start & (LANES - 1), shape)).astype(jnp.float32)
    pairs = [jnp.concatenate([a, b], axis=1) for a, b in zip(tiles[:-1], tiles[1:])]
    shifted = dot(jnp.concatenate(pairs, axis=0), chosen.astype(jnp.bfloat16))
    shifted = shifted.astype(jnp.bfloat16)
    return jnp.concatenate(
        [shifted[i * count : (i + 1) * count] for i in range(len(pairs))], axis=1
    )


def load_statistics(extended, start, length):
    tiles = nearest_tiles(extended, start, length)
    shape = tiles[0].shape
    for bit in range(LANES.bit_length() - 1):
        mask = bit_of(start, bit, shape, jnp.float32)
        tiles = [jnp.where(mask, pltpu.roll(t, LANES - (1 << bit), 1), t) for t in tiles]
    lane = lax.broadcasted_iota(jnp.int32, shape, 1)
    here = lane < LANES - jnp.broadcast_to(start & (LANES - 1), shape)
    return jnp.concatenate(
        [jnp.where(here, a, b) for a, b in zip(tiles[:-1], tiles[1:])], axis=1
    )


def split(x, terms):
    pieces = []
    for _ in range(terms):
        piece = x.astype(jnp.bfloat16)
        pieces.append(piece)
        x = x - piece.astype(jnp.float32)
    return pieces


def dot(a, b):
    return jnp.dot(a, b, preferred_element_type=jnp.float32)


def dot_lanes(a, b):
    return lax.dot_general(a, b, (((1,), (1,)), ((), ())), preferred_element_type=jnp.float32)


def dot_narrow(a, b):
    (a0, a1), (b0, b1) = split(a, 2), split(b, 2)
    return dot(a0, b0) + (dot(a0, b1) + dot(a1, b0))


def build_transform(lines, moments, active, transform, g, iterate, root, factor):
    blocks, _, runs, _ = lines.shape
    members = blocks * runs
    observed = jnp.concatenate([lines[b, g] for b in range(blocks)], axis=0).astype(jnp.float32)
    ens_mean = jnp.sum(observed, axis=0, keepdims=True) * (1.0 / members)
    anomaly = (observed - ens_mean).astype(jnp.bfloat16)
    weight = moments[1:2] * active
    rows = lax.broadcasted_iota(jnp.int32, (members, members), 0)
    lanes = lax.broadcasted_iota(jnp.int32, (members, members), 1)
    identity = (rows == lanes).astype(jnp.float32)
    weighted = split(anomaly.astype(jnp.float32) * weight, 2)
    gram = dot_lanes(anomaly, weighted[0]) + dot_lanes(anomaly, weighted[1])
    gram = gram + (members - 1) / inflation * identity
    innovation = jnp.broadcast_to(weight * (moments[0:1] - ens_mean), (16, weight.shape[1]))
    innovation = split(innovation, 3)
    innovation_sum = sum(dot_lanes(piece, anomaly) for piece in innovation)[0:1]
    squares = jnp.sum(jnp.sum(gram * gram, axis=0, keepdims=True), axis=1, keepdims=True)
    frobenius = jnp.sqrt(squares)
    iterate[...] = gram / frobenius
    factor[...] = 1.5 * identity - 0.5 * iterate[...]
    root[...] = factor[...]

    def step(i, carry):
        iterate[...] = dot_narrow(iterate[...], factor[...])
        factor[...] = 1.5 * identity - 0.5 * dot_narrow(root[...], iterate[...])
        root[...] = dot_narrow(factor[...], root[...])
        return carry

    lax.fori_loop(1, NS_ITERS, step, 0)
    inverse_root = root[...] / jnp.sqrt(frobenius)
    inner = jnp.sum(inverse_root * innovation_sum, axis=1, keepdims=True)
    mean_weight = jnp.sum(inverse_root * inner, axis=0, keepdims=True)
    turned = math.sqrt(members - 1) * inverse_root + mean_weight
    transform[g] = turned.astype(jnp.bfloat16)


def kernel(
    patch,
    groups,
    states_ref,
    runs_ref,
    stats_ref,
    starts_ref,
    active_ref,
    result_ref,
    packed,
    arrived,
    outgoing,
    received,
    extended,
    stats,
    all_starts,
    windows,
    lines,
    transform,
    joined,
    iterate,
    root,
    factor,
    send_sem,
    recv_sem,
    small_send,
    small_recv,
    halo_send,
    halo_recv,
):
    blocks, rows, _, _ = packed.shape
    length = lines.shape[3]
    own = runs_ref.shape[1]
    me = lax.axis_index("mem")
    region = lax.axis_index("reg")
    regions = lax.axis_size("reg")
    after = {"reg": lax.rem(region + 1, regions)}
    before = {"reg": lax.rem(region + regions - 1, regions)}
    peers = [lax.rem(me + k, blocks) for k in range(1, blocks)]

    def send(source, target, sems, device):
        copy = pltpu.make_async_remote_copy(
            src_ref=source,
            dst_ref=target,
            send_sem=sems[0],
            recv_sem=sems[1],
            device_id=device,
            device_id_type=MESH,
        )
        copy.start()
        return copy

    barrier = pltpu.get_barrier_semaphore()
    for device in [{"mem": peer} for peer in peers] + [after, before]:
        pl.semaphore_signal(barrier, inc=1, device_id=device, device_id_type=MESH)
    pl.semaphore_wait(barrier, blocks + 1)

    small = []
    for k, peer in enumerate(peers):
        sems = small_send.at[0, k], small_recv.at[0, k]
        small.append(send(starts_ref, all_starts.at[me], sems, {"mem": peer}))
    last_columns, first_columns = pl.ds(own - HW, HW), pl.ds(0, HW)
    beyond = pl.ds(own + HW, HW)
    for i, (source, target) in enumerate(((runs_ref, extended), (stats_ref, stats))):
        sems = halo_send.at[2 * i], halo_recv.at[2 * i]
        small.append(
            send(source.at[:, last_columns], target.at[:, first_columns], sems, after)
        )
        sems = halo_send.at[2 * i + 1], halo_recv.at[2 * i + 1]
        small.append(send(source.at[:, first_columns], target.at[:, beyond], sems, before))
    extended[:, HW : HW + own] = runs_ref[...]
    stats[:, HW : HW + own] = stats_ref[...]
    all_starts[me] = starts_ref[...]

    bounds = chunk_bounds(rows)
    forward = []

    def exchange_states(c):
        first, last = bounds[c]
        pack_rows(states_ref, packed, first, last)
        span = pl.ds(first, last - first)
        for k, peer in enumerate(peers):
            sems = send_sem.at[0, k, c], recv_sem.at[0, k, c]
            forward.append(
                send(packed.at[peer, span], arrived.at[me, span], sems, {"mem": peer})
            )
        arrived[me, span] = packed[me, span]

    exchange_states(0)
    for copy in small:
        copy.wait_recv()

    sent_windows = []
    for k, peer in enumerate(peers):

        def cut(g, carry, peer=peer):
            windows[peer, g] = load_runs(extended, all_starts[peer, pl.ds(g, 1), :], length)
            return carry

        lax.fori_loop(0, groups, cut, 0)
        sems = small_send.at[1, k], small_recv.at[1, k]
        sent_windows.append(send(windows.at[peer], lines.at[me], sems, {"mem": peer}))

    def cut_own(g, carry):
        lines[me, g] = load_runs(extended, starts_ref[pl.ds(g, 1), :], length)
        return carry

    lax.fori_loop(0, groups, cut_own, 0)
    for c in range(1, CHUNKS):
        exchange_states(c)
    for copy in sent_windows:
        copy.wait_recv()

    def build(g, carry):
        moments = load_statistics(stats, starts_ref[pl.ds(g, 1), :], length)
        active = active_ref[pl.ds(g, 1), :]
        build_transform(lines, moments, active, transform, g, iterate, root, factor)
        return carry

    lax.fori_loop(0, groups, build, 0)
    members = joined.shape[0]
    for g in range(groups):
        joined[:, g * members : (g + 1) * members] = transform[g]

    returned = []
    for c, (first, last) in enumerate(bounds):
        for copy in forward[c * (blocks - 1) : (c + 1) * (blocks - 1)]:
            copy.wait_recv()
        apply_rows(joined, arrived, outgoing, first, last, patch, groups)
        span = pl.ds(first, last - first)
        for k, peer in enumerate(peers):
            sems = send_sem.at[1, k, c], recv_sem.at[1, k, c]
            returned.append(
                send(outgoing.at[peer, span], received.at[me, span], sems, {"mem": peer})
            )
        received[me, span] = outgoing[me, span]
    for c, (first, last) in enumerate(bounds):
        for copy in returned[c * (blocks - 1) : (c + 1) * (blocks - 1)]:
            copy.wait_recv()
        unpack_rows(received, result_ref, first, last)
    for copy in small + sent_windows + forward + returned:
        copy.wait_send()


def assimilate(states, runs, statistics, starts, active, blocks, groups):
    fields, count, columns = states.shape
    members = count * blocks
    length = active.shape[1]
    own = runs.shape[1]
    width = columns // blocks
    rows = -(-fields // (LANES // width))
    packed = pltpu.VMEM((blocks, rows, count, LANES), jnp.bfloat16)
    square = pltpu.VMEM((members, members), jnp.float32)
    window = pltpu.VMEM((blocks, groups, count, length), jnp.bfloat16)
    dma = pltpu.SemaphoreType.DMA
    return pl.pallas_call(
        functools.partial(kernel, width // groups, groups),
        out_shape=jax.ShapeDtypeStruct(states.shape, jnp.bfloat16),
        in_specs=[pl.BlockSpec(memory_space=pltpu.VMEM)] * 5,
        out_specs=pl.BlockSpec(memory_space=pltpu.VMEM),
        scratch_shapes=[
            packed,
            packed,
            packed,
            packed,
            pltpu.VMEM((count, own + 2 * HW), jnp.bfloat16),
            pltpu.VMEM((statistics.shape[0], own + 2 * HW), jnp.float32),
            pltpu.VMEM((blocks,) + starts.shape, jnp.int32),
            window,
            window,
            pltpu.VMEM((groups, members, members), jnp.bfloat16),
            pltpu.VMEM((members, groups * members), jnp.bfloat16),
            square,
            square,
            square,
            dma((2, blocks - 1, CHUNKS)),
            dma((2, blocks - 1, CHUNKS)),
            dma((2, blocks - 1)),
            dma((2, blocks - 1)),
            dma((4,)),
            dma((4,)),
        ],
        compiler_params=pltpu.CompilerParams(
            collective_id=0, has_side_effects=True, vmem_limit_bytes=VMEM_LIMIT
        ),
        name="assimilate",
    )(states, runs, statistics, starts, active)


def per_device(
    prior_states,
    sensor_space_runs,
    sensor_readings,
    noise_precision,
    reading_pointers,
    reading_tally,
):
    blocks = lax.axis_size("mem")
    groups = reading_tally.shape[2]
    lists = reading_pointers[0, 0]
    length = lists.shape[1]
    starts = jnp.min(lists, axis=1)
    places = jnp.arange(length, dtype=jnp.int32)
    used = places[None, :] < reading_tally[0, 0][:, None]
    active = jnp.any(
        ((lists - starts[:, None])[:, :, None] == places[None, None, :]) & used[:, :, None], axis=1
    ).astype(jnp.float32)
    start_tile = jnp.broadcast_to(starts[:, None], (groups, LANES))
    start_tile = jnp.pad(start_tile, ((0, -groups % 8), (0, 0)))
    statistics = jnp.concatenate([sensor_readings, noise_precision])
    statistics = jnp.pad(statistics, ((0, 6), (0, 0)))
    analysed = assimilate(
        jnp.transpose(prior_states, (1, 0, 2)),
        sensor_space_runs[:, 0],
        statistics,
        start_tile,
        active,
        blocks,
        groups,
    )
    return jnp.transpose(analysed, (1, 0, 2))


def solution(mesh):
    placed = (
        P("mem", None, "reg"),
        P("mem", "reg", None),
        P("reg", None),
        P("reg", None),
        P("reg", "mem", None, None),
        P("reg", "mem", None),
    )
    return jax.shard_map(
        per_device, mesh=mesh, in_specs=placed, out_specs=P("mem", None, "reg"), check_vma=False
    )
```

time: 162 us -> 116 us (0.72)
  Pallas kernels: 65.4 us -> 105 us
  waiting for transfers between devices: 35.8 us -> 0 us
  matrix products: 15.4 us -> 0 us
  starting transfers between devices: 13.5 us -> 0 us
  blocking collectives: 8.23 us -> 0 us
  between operations: 8.17 us -> 0.02 us
  local copies, waits for them, and re-layouts: 10.2 us -> 5.41 us
    pallas_call x3 -> x1, Pallas kernels: 65.4 us -> 105 us  [assimilate(): pl.pallas_call(functools.partial(kernel, width // groups, groups), out_sh...]
    all_to_all x2 -> x0, waiting for transfers between devices: 35.8 us -> none  [the longest x1 24.1 us: per_device(): lax.all_to_all(packed, 'mem', split_axis=0, concat_axis=0, tiled=True)]
    dot_general x19 -> x0, matrix products: 15.4 us -> none  [the longest x5 3.73 us: local_transform(): factor = 1.5 * identity - 0.5 * dot(inverse_root, iterate)]
    all_to_all x2 -> x0, starting transfers between devices: 8.27 us -> none  [the longest x1 4.75 us: per_device(): lax.all_to_all(packed, 'mem', split_axis=0, concat_axis=0, tiled=True)]
    unnamed x1 -> x0, blocking collectives: 8.23 us -> none
    ppermute x4 -> x0, starting transfers between devices: 5.28 us -> none  [the longest x2 4.78 us: from_neighbours(): lax.ppermute(head, 'reg', [((i + 1) % count, i) for i in range(count)])]
    unnamed x12 -> x1, local copies, waits for them, and re-layouts: 7.42 us -> 4.74 us
  transfers between devices with their start and end apart: 6 -> 0, of which waited for: 2 -> 0; matrix products, arithmetic and copies ran while one was open for 15% -> 0% of each run, Pallas kernels for 9% -> 0%
where the time goes in v1:
time: 116 us
  Pallas kernels  105 us (91%)
  local copies, waits for them, and re-layouts  5.41 us (5%)
  other arithmetic  5.2 us (4%)
    pallas_call x1, Pallas kernels, assimilate(): pl.pallas_call(functools.partial(kernel, width // groups, groups), out_sh...  105 us
    unnamed x1, local copies, waits for them, and re-layouts  4.74 us

profile of v1, /device:TPU:0, one launch (start us, length us, event | category | flops | bytes accessed | tf_op | source)
XLA Modules:
  0.0 116.1 jit_solution(12095010920648657617)
XLA Ops:
  0.0 0.8 reduce_min.9
  0.8 0.7 iota_compare_fusion.2
  1.6 0.7 pad.12.starts_ref
  2.2 0.8 bitcast_subtract_fusion
  3.0 0.7 fusion.1
  3.7 0.6 convert_element_type.5.active_ref
  4.3 1.5 %select_maximum_fusion.stats_ref = f32[8,8192]{1,0:T(8,128)} fusion(f32[1,8192]{1,0:T(1,128)} %param.9, f32[1,8192]{1,0:T(1,128)} %param.8), kind=kLoop, calls=%fused_computation.3 | loop fusion | flops 262144 | bytes 327680 | tf_op jit(solution)/shard_map/concatenate | solution.py:439
  5.9 105.4 %assimilate.1 = bf16[227,64,128]{2,1,0:T(8,128)(2,1)} custom-call(bf16[227,64,128]{2,1,0:T(8,128)(2,1)} %bitcast.7, bf16[64,8192]{1,0:T(8,128)(2,1)} %bitcast.8, f32[8,8192]{1,0:T(8,128)} %select_maximum_fusion.stats_ref, s32[8,128]{1,0:T(8,128)} %pad.12.starts_ref, f32[4,512]{1,0:T(4,128)} %convert_element_type.5.active_ref), custom_call_target="tpu_custom_call" | custom-call | tf_op jit(solution)/shard_map/assimilate/pallas_call | solution.py:385
  111.3 4.7 %copy.8 = bf16[64,227,128]{2,0,1:T(8,128)(2,1)} copy(bf16[64,227,128]{2,0,1:T(8,128)(2,1)} %bitcast.6) | data formatting | bytes 7438336
  (1 shorter events, 0.0 us)

commit v2 on v1

--- a/solution.py
+++ b/solution.py
@@ -11,8 +11,8 @@
 NS_ITERS = 6
 HW = 256
 LANES = 128
-CHUNKS = 4
-VMEM_LIMIT = 60 * 1024 * 1024
+CHUNKS = 8
+VMEM_LIMIT = 48 * 1024 * 1024
 
 inflation = 1.1
 MESH = pl.DeviceIdType.MESH
@@ -37,7 +37,7 @@
 
 
 def chunk_bounds(rows):
-    edges = [rows * i // CHUNKS for i in range(CHUNKS + 1)]
+    edges = [rows * i // CHUNKS // 2 * 2 for i in range(CHUNKS)] + [rows]
     return list(zip(edges[:-1], edges[1:]))
 
 
@@ -187,44 +187,80 @@
 
 
 def dot_narrow(a, b):
-    (a0, a1), (b0, b1) = split(a, 2), split(b, 2)
-    return dot(a0, b0) + (dot(a0, b1) + dot(a1, b0))
-
-
-def build_transform(lines, moments, active, transform, g, iterate, root, factor):
+    return dot(a[0], b[0]) + (dot(a[0], b[1]) + dot(a[1], b[0]))
+
+
+def used_positions(lists_ref, tally_ref, start, g):
+    length = lists_ref.shape[1]
+    shape = (length, length)
+    tallies = tally_ref[...].astype(jnp.float32)
+    lane = lax.broadcasted_iota(jnp.int32, tallies.shape, 1)
+    tally = jnp.sum(jnp.where(lane == g, tallies, 0.0), axis=1, keepdims=True)
+    place = lists_ref[pl.ds(g, 1), :] - jnp.concatenate([start] * (length // LANES), axis=1)
+    listed = lax.broadcasted_iota(jnp.int32, shape, 0) == jnp.broadcast_to(place, shape)
+    listed = listed.astype(jnp.float32).astype(jnp.bfloat16)
+    entry = lax.broadcasted_iota(jnp.int32, (16, length), 1).astype(jnp.float32)
+    used = (entry < tally).astype(jnp.float32).astype(jnp.bfloat16)
+    return dot_lanes(used, listed)[0:1]
+
+
+def identity_of(members):
+    rows = lax.broadcasted_iota(jnp.int32, (members, members), 0)
+    lanes = lax.broadcasted_iota(jnp.int32, (members, members), 1)
+    return (rows == lanes).astype(jnp.float32)
+
+
+def begin_root(lines, readings, weight, g, iterate, root, factor, innovation_sum, norm):
     blocks, _, runs, _ = lines.shape
     members = blocks * runs
     observed = jnp.concatenate([lines[b, g] for b in range(blocks)], axis=0).astype(jnp.float32)
     ens_mean = jnp.sum(observed, axis=0, keepdims=True) * (1.0 / members)
     anomaly = (observed - ens_mean).astype(jnp.bfloat16)
-    weight = moments[1:2] * active
-    rows = lax.broadcasted_iota(jnp.int32, (members, members), 0)
-    lanes = lax.broadcasted_iota(jnp.int32, (members, members), 1)
-    identity = (rows == lanes).astype(jnp.float32)
+    identity = identity_of(members)
     weighted = split(anomaly.astype(jnp.float32) * weight, 2)
     gram = dot_lanes(anomaly, weighted[0]) + dot_lanes(anomaly, weighted[1])
     gram = gram + (members - 1) / inflation * identity
-    innovation = jnp.broadcast_to(weight * (moments[0:1] - ens_mean), (16, weight.shape[1]))
+    innovation = jnp.broadcast_to(weight * (readings - ens_mean), (16, weight.shape[1]))
     innovation = split(innovation, 3)
-    innovation_sum = sum(dot_lanes(piece, anomaly) for piece in innovation)[0:1]
+    innovation_sum[g] = sum(dot_lanes(piece, anomaly) for piece in innovation)[0:8]
     squares = jnp.sum(jnp.sum(gram * gram, axis=0, keepdims=True), axis=1, keepdims=True)
     frobenius = jnp.sqrt(squares)
-    iterate[...] = gram / frobenius
-    factor[...] = 1.5 * identity - 0.5 * iterate[...]
-    root[...] = factor[...]
+    norm[g] = jnp.broadcast_to(jnp.sqrt(frobenius), norm.shape[1:])
+    scaled = gram / frobenius
+    first = 1.5 * identity - 0.5 * scaled
+    keep(iterate, g, scaled)
+    keep(factor, g, first)
+    keep(root, g, first)
+
+
+def keep(ref, g, value):
+    ref[g, 0], ref[g, 1] = split(value, 2)
+
+
+def refine_roots(iterate, root, factor):
+    groups, _, members, _ = iterate.shape
 
     def step(i, carry):
-        iterate[...] = dot_narrow(iterate[...], factor[...])
-        factor[...] = 1.5 * identity - 0.5 * dot_narrow(root[...], iterate[...])
-        root[...] = dot_narrow(factor[...], root[...])
+        for g in range(groups):
+            keep(iterate, g, dot_narrow(iterate[g], factor[g]))
+        for g in range(groups):
+            product = dot_narrow(root[g], iterate[g])
+            keep(factor, g, 1.5 * identity_of(members) - 0.5 * product)
+        for g in range(groups):
+            keep(root, g, dot_narrow(factor[g], root[g]))
         return carry
 
     lax.fori_loop(1, NS_ITERS, step, 0)
-    inverse_root = root[...] / jnp.sqrt(frobenius)
-    inner = jnp.sum(inverse_root * innovation_sum, axis=1, keepdims=True)
+
+
+def finish_transform(root, innovation_sum, norm, joined, g):
+    members = root.shape[2]
+    inverse_root = root[g, 0].astype(jnp.float32) + root[g, 1].astype(jnp.float32)
+    inverse_root = inverse_root * (1.0 / norm[g][0:1, 0:1])
+    inner = jnp.sum(inverse_root * innovation_sum[g][0:1], axis=1, keepdims=True)
     mean_weight = jnp.sum(inverse_root * inner, axis=0, keepdims=True)
     turned = math.sqrt(members - 1) * inverse_root + mean_weight
-    transform[g] = turned.astype(jnp.bfloat16)
+    joined[:, g * members : (g + 1) * members] = turned.astype(jnp.bfloat16)
 
 
 def kernel(
@@ -232,24 +268,28 @@
     groups,
     states_ref,
     runs_ref,
-    stats_ref,
-    starts_ref,
-    active_ref,
+    readings_ref,
+    precision_ref,
+    lists_ref,
+    tally_ref,
     result_ref,
     packed,
     arrived,
     outgoing,
     received,
     extended,
-    stats,
+    readings,
+    precision,
+    starts,
     all_starts,
     windows,
     lines,
-    transform,
     joined,
     iterate,
     root,
     factor,
+    innovation_sum,
+    norm,
     send_sem,
     recv_sem,
     small_send,
@@ -279,6 +319,10 @@
         copy.start()
         return copy
 
+    lowest = jnp.min(lists_ref[...].astype(jnp.float32), axis=1, keepdims=True)
+    starts[...] = jnp.zeros_like(starts)
+    starts[0:groups, :] = jnp.broadcast_to(lowest, (groups, LANES)).astype(jnp.int32)
+
     barrier = pltpu.get_barrier_semaphore()
     for device in [{"mem": peer} for peer in peers] + [after, before]:
         pl.semaphore_signal(barrier, inc=1, device_id=device, device_id_type=MESH)
@@ -287,10 +331,12 @@
     small = []
     for k, peer in enumerate(peers):
         sems = small_send.at[0, k], small_recv.at[0, k]
-        small.append(send(starts_ref, all_starts.at[me], sems, {"mem": peer}))
+        small.append(send(starts, all_starts.at[me], sems, {"mem": peer}))
     last_columns, first_columns = pl.ds(own - HW, HW), pl.ds(0, HW)
     beyond = pl.ds(own + HW, HW)
-    for i, (source, target) in enumerate(((runs_ref, extended), (stats_ref, stats))):
+    for i, (source, target) in enumerate(
+        ((runs_ref, extended), (readings_ref, readings), (precision_ref, precision))
+    ):
         sems = halo_send.at[2 * i], halo_recv.at[2 * i]
         small.append(
             send(source.at[:, last_columns], target.at[:, first_columns], sems, after)
@@ -298,8 +344,8 @@
         sems = halo_send.at[2 * i + 1], halo_recv.at[2 * i + 1]
         small.append(send(source.at[:, first_columns], target.at[:, beyond], sems, before))
     extended[:, HW : HW + own] = runs_ref[...]
-    stats[:, HW : HW + own] = stats_ref[...]
-    all_starts[me] = starts_ref[...]
+    readings[:, HW : HW + own] = readings_ref[...]
+    precision[:, HW : HW + own] = precision_ref[...]
 
     bounds = chunk_bounds(rows)
     forward = []
@@ -331,7 +377,7 @@
         sent_windows.append(send(windows.at[peer], lines.at[me], sems, {"mem": peer}))
 
     def cut_own(g, carry):
-        lines[me, g] = load_runs(extended, starts_ref[pl.ds(g, 1), :], length)
+        lines[me, g] = load_runs(extended, starts[pl.ds(g, 1), :], length)
         return carry
 
     lax.fori_loop(0, groups, cut_own, 0)
@@ -340,16 +386,18 @@
     for copy in sent_windows:
         copy.wait_recv()
 
-    def build(g, carry):
-        moments = load_statistics(stats, starts_ref[pl.ds(g, 1), :], length)
-        active = active_ref[pl.ds(g, 1), :]
-        build_transform(lines, moments, active, transform, g, iterate, root, factor)
+    def begin(g, carry):
+        start = starts[pl.ds(g, 1), :]
+        weight = load_statistics(precision, start, length)
+        weight = weight * used_positions(lists_ref, tally_ref, start, g)
+        observed = load_statistics(readings, start, length)
+        begin_root(lines, observed, weight, g, iterate, root, factor, innovation_sum, norm)
         return carry
 
-    lax.fori_loop(0, groups, build, 0)
-    members = joined.shape[0]
+    lax.fori_loop(0, groups, begin, 0)
+    refine_roots(iterate, root, factor)
     for g in range(groups):
-        joined[:, g * members : (g + 1) * members] = transform[g]
+        finish_transform(root, innovation_sum, norm, joined, g)
 
     returned = []
     for c, (first, last) in enumerate(bounds):
@@ -371,21 +419,22 @@
         copy.wait_send()
 
 
-def assimilate(states, runs, statistics, starts, active, blocks, groups):
+def assimilate(states, runs, readings, precision, lists, tally, blocks):
     fields, count, columns = states.shape
+    groups, length = lists.shape
     members = count * blocks
-    length = active.shape[1]
     own = runs.shape[1]
     width = columns // blocks
     rows = -(-fields // (LANES // width))
     packed = pltpu.VMEM((blocks, rows, count, LANES), jnp.bfloat16)
-    square = pltpu.VMEM((members, members), jnp.float32)
+    square = pltpu.VMEM((groups, 2, members, members), jnp.bfloat16)
     window = pltpu.VMEM((blocks, groups, count, length), jnp.bfloat16)
+    start_rows = groups + -groups % 8
     dma = pltpu.SemaphoreType.DMA
     return pl.pallas_call(
         functools.partial(kernel, width // groups, groups),
-        out_shape=jax.ShapeDtypeStruct(states.shape, jnp.bfloat16),
-        in_specs=[pl.BlockSpec(memory_space=pltpu.VMEM)] * 5,
+        out_shape=pltpu.VMEM(states.shape, jnp.bfloat16),
+        in_specs=[pl.BlockSpec(memory_space=pltpu.VMEM)] * 6,
         out_specs=pl.BlockSpec(memory_space=pltpu.VMEM),
         scratch_shapes=[
             packed,
@@ -393,27 +442,30 @@
             packed,
             packed,
             pltpu.VMEM((count, own + 2 * HW), jnp.bfloat16),
-            pltpu.VMEM((statistics.shape[0], own + 2 * HW), jnp.float32),
-            pltpu.VMEM((blocks,) + starts.shape, jnp.int32),
+            pltpu.VMEM((1, own + 2 * HW), jnp.float32),
+            pltpu.VMEM((1, own + 2 * HW), jnp.float32),
+            pltpu.VMEM((start_rows, LANES), jnp.int32),
+            pltpu.VMEM((blocks, start_rows, LANES), jnp.int32),
             window,
             window,
-            pltpu.VMEM((groups, members, members), jnp.bfloat16),
             pltpu.VMEM((members, groups * members), jnp.bfloat16),
             square,
             square,
             square,
+            pltpu.VMEM((groups, 8, members), jnp.float32),
+            pltpu.VMEM((groups, 8, LANES), jnp.float32),
             dma((2, blocks - 1, CHUNKS)),
             dma((2, blocks - 1, CHUNKS)),
             dma((2, blocks - 1)),
             dma((2, blocks - 1)),
-            dma((4,)),
-            dma((4,)),
+            dma((6,)),
+            dma((6,)),
         ],
         compiler_params=pltpu.CompilerParams(
             collective_id=0, has_side_effects=True, vmem_limit_bytes=VMEM_LIMIT
         ),
         name="assimilate",
-    )(states, runs, statistics, starts, active)
+    )(states, runs, readings, precision, lists, tally)
 
 
 def per_device(
@@ -424,28 +476,14 @@
     reading_pointers,
     reading_tally,
 ):
-    blocks = lax.axis_size("mem")
-    groups = reading_tally.shape[2]
-    lists = reading_pointers[0, 0]
-    length = lists.shape[1]
-    starts = jnp.min(lists, axis=1)
-    places = jnp.arange(length, dtype=jnp.int32)
-    used = places[None, :] < reading_tally[0, 0][:, None]
-    active = jnp.any(
-        ((lists - starts[:, None])[:, :, None] == places[None, None, :]) & used[:, :, None], axis=1
-    ).astype(jnp.float32)
-    start_tile = jnp.broadcast_to(starts[:, None], (groups, LANES))
-    start_tile = jnp.pad(start_tile, ((0, -groups % 8), (0, 0)))
-    statistics = jnp.concatenate([sensor_readings, noise_precision])
-    statistics = jnp.pad(statistics, ((0, 6), (0, 0)))
     analysed = assimilate(
         jnp.transpose(prior_states, (1, 0, 2)),
         sensor_space_runs[:, 0],
-        statistics,
-        start_tile,
-        active,
-        blocks,
-        groups,
+        sensor_readings,
+        noise_precision,
+        reading_pointers[0, 0],
+        reading_tally[0],
+        lax.axis_size("mem"),
     )
     return jnp.transpose(analysed, (1, 0, 2))
 

time: 116 us -> 108 us (0.931)
  other arithmetic: 5.2 us -> 0 us
  Pallas kernels: 105 us -> 102 us
    pallas_call x1, Pallas kernels: 105 us -> 102 us  [assimilate(): pl.pallas_call(functools.partial(kernel, width // groups, groups), out_sh...]
    concatenate x1 -> x0, other arithmetic: 1.55 us -> none  [per_device(): statistics = jnp.concatenate([sensor_readings, noise_precision])]
    unnamed x1 -> x11, local copies, waits for them, and re-layouts: 4.74 us -> 5.95 us
where the time goes in v2:
time: 108 us
  Pallas kernels  102 us (94%)
  local copies, waits for them, and re-layouts  5.95 us (6%)
    pallas_call x1, Pallas kernels, assimilate(): pl.pallas_call(functools.partial(kernel, width // groups, groups), out_sh...  102 us
    unnamed x11, local copies, waits for them, and re-layouts  5.95 us

profile of v2, /device:TPU:0, one launch (start us, length us, event | category | flops | bytes accessed | tf_op | source)
XLA Modules:
  0.0 108.1 jit_solution(10609748680711243161)
XLA Ops:
  0.0 0.0 copy-start
  0.0 1.2 %copy-done = bf16[64,1,8192]{2,0,1:T(8,128)(2,1)S(1)} copy-done((bf16[64,1,8192]{2,0,1:T(8,128)(2,1)S(1)}, bf16[64,1,8192]{2,0,1:T(8,128)(2,1)}, u32[]{:S(2)}) %copy-start) | copy-done | bytes 1048600
  1.2 0.0 copy-start.1
  1.2 0.8 copy-done.1
  2.0 0.0 copy-start.2
  2.0 0.8 copy-done.2
  2.7 0.0 copy-start.3
  2.7 0.7 copy-done.3
  3.4 0.0 copy-start.4
  3.4 0.7 copy-done.4
  4.1 102.1 %assimilate.1 = bf16[227,64,128]{2,1,0:T(8,128)(2,1)S(1)} custom-call(bf16[227,64,128]{2,1,0:T(8,128)(2,1)} %bitcast.9, bf16[64,8192]{1,0:T(8,128)(2,1)S(1)} %bitcast.6, f32[1,8192]{1,0:T(1,128)S(1)} %copy-done.1, f32[1,8192]{1,0:T(1,128)S(1)} %copy-done.2, s32[4,512]{1,0:T(4,128)S(1)} %bitcast.7, s32[1,4]{1,0:T(1,128)S(1)} %bitcast.8), custom_call_target="tpu_custom_call" | custom-call | tf_op jit(solution)/shard_map/assimilate/pallas_call | solution.py:434
  106.2 1.9 %copy.8 = bf16[64,227,128]{2,0,1:T(8,128)(2,1)} copy(bf16[64,227,128]{2,0,1:T(8,128)(2,1)S(1)} %bitcast.5) | data formatting | bytes 7438336
Async XLA Ops:
  0.0 1.2 %copy-start = (bf16[64,1,8192]{2,0,1:T(8,128)(2,1)S(1)}, bf16[64,1,8192]{2,0,1:T(8,128)(2,1)}, u32[]{:S(2)}) copy-start(bf16[64,1,8192]{2,0,1:T(8,128)(2,1)} %param.7) | copy-start | bytes 3145732
  1.2 0.8 copy-start.1
  2.0 0.8 copy-start.2
  2.7 0.7 copy-start.3
  3.4 0.7 copy-start.4

commit v3 on v2

--- a/solution.py
+++ b/solution.py
@@ -266,13 +266,16 @@
 def kernel(
     patch,
     groups,
+    states_hbm,
+    runs_hbm,
+    readings_hbm,
+    precision_hbm,
+    lists_hbm,
+    tally_hbm,
+    result_ref,
     states_ref,
-    runs_ref,
-    readings_ref,
-    precision_ref,
     lists_ref,
     tally_ref,
-    result_ref,
     packed,
     arrived,
     outgoing,
@@ -296,10 +299,12 @@
     small_recv,
     halo_send,
     halo_recv,
+    local_sem,
 ):
     blocks, rows, _, _ = packed.shape
     length = lines.shape[3]
-    own = runs_ref.shape[1]
+    own = runs_hbm.shape[1]
+    own_columns = pl.ds(HW, own)
     me = lax.axis_index("mem")
     region = lax.axis_index("reg")
     regions = lax.axis_size("reg")
@@ -319,13 +324,27 @@
         copy.start()
         return copy
 
+    barrier = pltpu.get_barrier_semaphore()
+    for device in [{"mem": peer} for peer in peers] + [after, before]:
+        pl.semaphore_signal(barrier, inc=1, device_id=device, device_id_type=MESH)
+    local = []
+    for i, (source, target) in enumerate(
+        (
+            (lists_hbm, lists_ref),
+            (tally_hbm, tally_ref),
+            (states_hbm, states_ref),
+            (runs_hbm, extended.at[:, own_columns]),
+            (readings_hbm, readings.at[:, own_columns]),
+            (precision_hbm, precision.at[:, own_columns]),
+        )
+    ):
+        copy = pltpu.make_async_copy(source, target, local_sem.at[i])
+        copy.start()
+        local.append(copy)
+    local[0].wait()
     lowest = jnp.min(lists_ref[...].astype(jnp.float32), axis=1, keepdims=True)
     starts[...] = jnp.zeros_like(starts)
     starts[0:groups, :] = jnp.broadcast_to(lowest, (groups, LANES)).astype(jnp.int32)
-
-    barrier = pltpu.get_barrier_semaphore()
-    for device in [{"mem": peer} for peer in peers] + [after, before]:
-        pl.semaphore_signal(barrier, inc=1, device_id=device, device_id_type=MESH)
     pl.semaphore_wait(barrier, blocks + 1)
 
     small = []
@@ -335,7 +354,7 @@
     last_columns, first_columns = pl.ds(own - HW, HW), pl.ds(0, HW)
     beyond = pl.ds(own + HW, HW)
     for i, (source, target) in enumerate(
-        ((runs_ref, extended), (readings_ref, readings), (precision_ref, precision))
+        ((runs_hbm, extended), (readings_hbm, readings), (precision_hbm, precision))
     ):
         sems = halo_send.at[2 * i], halo_recv.at[2 * i]
         small.append(
@@ -343,16 +362,13 @@
         )
         sems = halo_send.at[2 * i + 1], halo_recv.at[2 * i + 1]
         small.append(send(source.at[:, first_columns], target.at[:, beyond], sems, before))
-    extended[:, HW : HW + own] = runs_ref[...]
-    readings[:, HW : HW + own] = readings_ref[...]
-    precision[:, HW : HW + own] = precision_ref[...]
+    local[2].wait()
 
     bounds = chunk_bounds(rows)
     forward = []
 
-    def exchange_states(c):
+    def send_states(c):
         first, last = bounds[c]
-        pack_rows(states_ref, packed, first, last)
         span = pl.ds(first, last - first)
         for k, peer in enumerate(peers):
             sems = send_sem.at[0, k, c], recv_sem.at[0, k, c]
@@ -361,7 +377,10 @@
             )
         arrived[me, span] = packed[me, span]
 
-    exchange_states(0)
+    pack_rows(states_ref, packed, *bounds[0])
+    send_states(0)
+    for copy in local[1:2] + local[3:]:
+        copy.wait()
     for copy in small:
         copy.wait_recv()
 
@@ -381,10 +400,11 @@
         return carry
 
     lax.fori_loop(0, groups, cut_own, 0)
-    for c in range(1, CHUNKS):
-        exchange_states(c)
+    pack_rows(states_ref, packed, bounds[0][1], rows)
     for copy in sent_windows:
         copy.wait_recv()
+    for c in range(1, CHUNKS):
+        send_states(c)
 
     def begin(g, carry):
         start = starts[pl.ds(g, 1), :]
@@ -434,9 +454,12 @@
     return pl.pallas_call(
         functools.partial(kernel, width // groups, groups),
         out_shape=pltpu.VMEM(states.shape, jnp.bfloat16),
-        in_specs=[pl.BlockSpec(memory_space=pltpu.VMEM)] * 6,
+        in_specs=[pl.BlockSpec(memory_space=pltpu.HBM)] * 6,
         out_specs=pl.BlockSpec(memory_space=pltpu.VMEM),
         scratch_shapes=[
+            pltpu.VMEM(states.shape, jnp.bfloat16),
+            pltpu.VMEM(lists.shape, jnp.int32),
+            pltpu.VMEM(tally.shape, jnp.int32),
             packed,
             packed,
             packed,
@@ -460,12 +483,18 @@
             dma((2, blocks - 1)),
             dma((6,)),
             dma((6,)),
+            dma((6,)),
         ],
         compiler_params=pltpu.CompilerParams(
             collective_id=0, has_side_effects=True, vmem_limit_bytes=VMEM_LIMIT
         ),
         name="assimilate",
-    )(states, runs, readings, precision, lists, tally)
+    )(
+        *(
+            pltpu.with_memory_space_constraint(operand, pltpu.HBM)
+            for operand in (states, runs, readings, precision, lists, tally)
+        )
+    )
 
 
 def per_device(

time: 108 us -> 104 us (0.963)
  local copies, waits for them, and re-layouts: 5.95 us -> 1.86 us
    unnamed x11 -> x1, local copies, waits for them, and re-layouts: 5.95 us -> 1.86 us
where the time goes in v3:
time: 104 us
  Pallas kernels  102 us (98%)
  local copies, waits for them, and re-layouts  1.86 us (2%)
    pallas_call x1, Pallas kernels, assimilate(): pl.pallas_call(functools.partial(kernel, width // groups, groups), out_sh...  102 us

profile of v3, /device:TPU:0, one launch (start us, length us, event | category | flops | bytes accessed | tf_op | source)
XLA Modules:
  0.0 103.8 jit_solution(8750582787330683185)
XLA Ops:
  0.0 102.0 %assimilate.1 = bf16[227,64,128]{2,1,0:T(8,128)(2,1)S(1)} custom-call(bf16[227,64,128]{2,1,0:T(8,128)(2,1)} %bitcast.6, bf16[64,8192]{1,0:T(8,128)(2,1)} %bitcast.7, f32[1,8192]{1,0:T(1,128)} %readings_hbm.1, f32[1,8192]{1,0:T(1,128)} %precision_hbm.1, s32[4,512]{1,0:T(4,128)} %bitcast.8, s32[1,4]{1,0:T(1,128)} %bitcast.9), custom_call_target="tpu_custom_call" | custom-call | tf_op jit(solution)/shard_map/assimilate/pallas_call | solution.py:454
  102.0 1.9 %copy.8 = bf16[64,227,128]{2,0,1:T(8,128)(2,1)} copy(bf16[64,227,128]{2,0,1:T(8,128)(2,1)S(1)} %bitcast.5) | data formatting | bytes 7438336

commit v4 on v3

--- a/solution.py
+++ b/solution.py
@@ -12,6 +12,7 @@
 HW = 256
 LANES = 128
 CHUNKS = 8
+EARLY = 2
 VMEM_LIMIT = 48 * 1024 * 1024
 
 inflation = 1.1
@@ -367,8 +368,9 @@
     bounds = chunk_bounds(rows)
     forward = []
 
-    def send_states(c):
+    def exchange_states(c):
         first, last = bounds[c]
+        pack_rows(states_ref, packed, first, last)
         span = pl.ds(first, last - first)
         for k, peer in enumerate(peers):
             sems = send_sem.at[0, k, c], recv_sem.at[0, k, c]
@@ -377,8 +379,8 @@
             )
         arrived[me, span] = packed[me, span]
 
-    pack_rows(states_ref, packed, *bounds[0])
-    send_states(0)
+    for c in range(EARLY):
+        exchange_states(c)
     for copy in local[1:2] + local[3:]:
         copy.wait()
     for copy in small:
@@ -400,11 +402,10 @@
         return carry
 
     lax.fori_loop(0, groups, cut_own, 0)
-    pack_rows(states_ref, packed, bounds[0][1], rows)
+    for c in range(EARLY, CHUNKS):
+        exchange_states(c)
     for copy in sent_windows:
         copy.wait_recv()
-    for c in range(1, CHUNKS):
-        send_states(c)
 
     def begin(g, carry):
         start = starts[pl.ds(g, 1), :]

time: 104 us -> 103 us (level)
    pallas_call x1, Pallas kernels: 102 us -> 101 us  [assimilate(): pl.pallas_call(functools.partial(kernel, width // groups, groups), out_sh...]
where the time goes in v4:
time: 103 us; the launch traced here: 102 us
  Pallas kernels  101 us (98%)
  local copies, waits for them, and re-layouts  1.86 us (2%)
    pallas_call x1, Pallas kernels, assimilate(): pl.pallas_call(functools.partial(kernel, width // groups, groups), out_sh...  101 us

profile of v4, /device:TPU:0, one launch (start us, length us, event | category | flops | bytes accessed | tf_op | source)
XLA Modules:
  0.0 102.4 jit_solution(16092872887247602482)
XLA Ops:
  0.0 100.5 %assimilate.1 = bf16[227,64,128]{2,1,0:T(8,128)(2,1)S(1)} custom-call(bf16[227,64,128]{2,1,0:T(8,128)(2,1)} %bitcast.6, bf16[64,8192]{1,0:T(8,128)(2,1)} %bitcast.7, f32[1,8192]{1,0:T(1,128)} %readings_hbm.1, f32[1,8192]{1,0:T(1,128)} %precision_hbm.1, s32[4,512]{1,0:T(4,128)} %bitcast.8, s32[1,4]{1,0:T(1,128)} %bitcast.9), custom_call_target="tpu_custom_call" | custom-call | tf_op jit(solution)/shard_map/assimilate/pallas_call | solution.py:455
  100.5 1.9 %copy.8 = bf16[64,227,128]{2,0,1:T(8,128)(2,1)} copy(bf16[64,227,128]{2,0,1:T(8,128)(2,1)S(1)} %bitcast.5) | data formatting | bytes 7438336
